TPU v7x, 256 devices: a whole 4x4x8 slice. The times are simulated.
256 devices in a mesh: blk: 16 (over x_hi, y, core), grp: 16 (over x_lo, z).
Axes of the slice: x: 4 (x_hi: 2, x_lo: 2; x = x_hi * 2 + x_lo), y: 4, z: 8, core: 2. Of those that a mesh axis runs over, the one named last changes fastest.
Arguments:
- features: bfloat16 [16, 16, 640, 256], P('blk', 'grp'), may hold values from -6 to 6
- tiles: bfloat16 [16, 16, 8, 640, 640], P('blk', 'grp'), as said below
- slot_columns: int32 [16, 16, 8], P('blk', 'grp'), may hold values from 0 to 15, as said below
- slot_counts: int32 [16, 16], P('blk', 'grp'), may hold values from 2 to 8, as said below
- weight: bfloat16 [256, 256], replicated, may hold values from -0.375 to 0.375
- out_grad: bfloat16 [16, 16, 640, 256], P('blk', 'grp'), may hold values from -6 to 6
Outputs:
- layer_output: bfloat16 [16, 16, 640, 256], P('blk', 'grp')
- feature_grad: bfloat16 [16, 16, 640, 256], P('blk', 'grp')
- weight_grad: float32 [256, 256], replicated
Inputs may be any that keep to these rules, and one draw needn't show every extreme that they name: `slot_columns`: slot 0 of row block b names b itself; the next slot_counts - 1 slots name distinct other blocks of the same graph in ascending order; unused slots name b. The block pattern is symmetric: row block b names c exactly when row block c names b. `slot_counts`: in every graph one row block uses all 8 slots. `tiles`: for active slots: when row block b names c != b, the tile of row block c that names b is the transpose of b's tile; the tile of slot 0 is symmetric.
All inputs are finite; a program needn't handle non-finite values.
Results may differ from a plain program's by a relative error of at most 0.015.
Values may be sent and summed in bfloat16 or wider, within the bound.
A program may use at most 64 MiB of HBM per device.

v0:
```python
import math

import jax
import jax.numpy as jnp
from jax import lax
from jax.sharding import PartitionSpec as P


def silu_slope(linear):
    sigmoid_v = jax.nn.sigmoid(linear)
    return sigmoid_v * (1.0 + linear * (1.0 - sigmoid_v))


def fold_slots(own_tiles, columns, live_count, running, pieces):
    piece_count = pieces.shape[0]

    def fold_slot_step(slot, total):
        offset = columns[slot]
        active = (slot < live_count) & (offset >= 0) & (offset < piece_count)

        def fold_accumulate(current):
            target = jnp.clip(offset, 0, piece_count - 1)
            panel = lax.dynamic_index_in_dim(pieces, target, 0, keepdims=False)[0]
            return current + jnp.dot(own_tiles[slot], panel, preferred_element_type=jnp.float32)

        return lax.cond(active, fold_accumulate, lambda current: current, total)

    return lax.fori_loop(0, own_tiles.shape[0], fold_slot_step, running)


def per_device(features, tiles, slot_columns, slot_counts, weight, out_grad):
    row_count = features.shape[2]
    feat_width = features.shape[3]
    out_width = weight.shape[1]
    own_tiles = tiles[0, 0]
    columns = slot_columns[0, 0]
    live_count = slot_counts[0, 0]
    zero_panel = jnp.zeros((row_count, feat_width), jnp.float32)
    summed = fold_slots(
        own_tiles,
        columns,
        live_count,
        zero_panel,
        lax.all_gather(features, "blk", axis=0, tiled=True),
    ).astype(jnp.bfloat16)
    linear = jnp.dot(summed, weight, preferred_element_type=jnp.float32)
    layer_output = jax.nn.silu(linear).astype(jnp.bfloat16).reshape(1, 1, row_count, out_width)
    slope_grad = (out_grad[0, 0].astype(jnp.float32) * silu_slope(linear)).astype(jnp.bfloat16)
    partial_value = lax.dot_general(
        summed, slope_grad, (((0,), (0,)), ((), ())), preferred_element_type=jnp.float32
    )
    panel_grad = lax.dot_general(
        slope_grad, weight, (((1,), (1,)), ((), ())), preferred_element_type=jnp.float32
    ).astype(jnp.bfloat16)
    blocks = row_count * lax.axis_size("blk") // row_count

    def adjoint_slot_step(slot, total):
        offset = columns[slot]
        active = (slot < live_count) & (offset >= 0) & (offset < blocks)

        def adjoint_accumulate(current):
            target = jnp.clip(offset, 0, blocks - 1)
            product = lax.dot_general(
                own_tiles[slot],
                panel_grad,
                (((0,), (0,)), ((), ())),
                preferred_element_type=jnp.float32,
            )
            present = lax.dynamic_index_in_dim(current, target, 0, keepdims=False)
            return lax.dynamic_update_index_in_dim(current, present + product, target, 0)

        return lax.cond(active, adjoint_accumulate, lambda current: current, total)

    zero_terms = jnp.zeros((blocks, row_count, feat_width), jnp.float32)
    totals = lax.fori_loop(0, own_tiles.shape[0], adjoint_slot_step, zero_terms)
    grad_rows = lax.psum_scatter(
        totals.reshape(row_count * lax.axis_size("blk"), feat_width).astype(jnp.bfloat16),
        "blk",
        scatter_dimension=0,
        tiled=True,
    )
    feature_grad = grad_rows.reshape(1, 1, row_count, feat_width)
    weight_total = lax.psum(partial_value, ("blk", "grp"))
    node_total = row_count * lax.axis_size("blk") * lax.axis_size("grp")
    weight_grad = weight_total * (1.0 / math.sqrt(node_total))
    return (layer_output, feature_grad, weight_grad)


def solution(mesh):
    in_specs = (
        P("blk", "grp", None, None),
        P("blk", "grp", None, None, None),
        P("blk", "grp", None),
        P("blk", "grp"),
        P(),
        P("blk", "grp", None, None),
    )
    out_specs = (P("blk", "grp", None, None), P("blk", "grp", None, None), P())
    return jax.shard_map(
        per_device, mesh=mesh, in_specs=in_specs, out_specs=out_specs, check_vma=False
    )
```

profile of v0, /device:TPU:1, one launch (start us, length us, event | category | flops | bytes accessed | tf_op | source)
XLA Modules:
  0.0 475.9 jit_solution(9859559427187938123)
XLA Ops:
  8.0 71.9 %all-gather.2.cloned.1.call-done = bf16[16,1,640,256]{3,2,1,0:T(8,128)(2,1)} async-done(((bf16[1,1,640,256]{3,2,1,0:T(8,128)(2,1)}), bf16[16,1,640,256]{3,2,1,0:T(8,128)(2,1)}) %all-gather.2.cloned.1.call-update) | async-done | bytes 5242896 | tf_op jit(solution)/shard_map/all_gather | solution.py:44
  79.9 32.8 %while.32 = (s32[]{:T(128)}, f32[640,256]{1,0:T(8,128)S(1)}, s32[]{:T(128)}, s32[8]{0:T(128)}, bf16[8,640,640]{2,1,0:T(8,128)(2,1)}, /*index=5*/bf16[16,1,640,25...) while((s32[]{:T(128)}, f32[640,256]{1,0:T(8,128)S(1)}, s32[]{:T(128)}, s32[8]{0:T(128)}, ...), condition=%wide.region_3.4_spmd, body=%wide.region_0.3_spmd.sunk | while | flops 209879040 | bytes 2457857 | solution.py:28
  79.9 1.2 dynamic_slice.43
  83.1 2.3 conditional.4
  83.8 1.7 convolution_add_fusion
  85.5 1.2 dynamic_slice.43
  88.7 2.3 conditional.4
  89.3 1.7 convolution_add_fusion
  91.0 1.2 dynamic_slice.43
  94.2 2.3 conditional.4
  94.9 1.7 convolution_add_fusion
  96.6 1.2 dynamic_slice.43
  99.8 1.2 dynamic_slice.43
  103.0 1.2 dynamic_slice.43
  106.3 1.2 dynamic_slice.43
  109.5 1.2 dynamic_slice.43
  112.7 1.2 fusion.10
  115.3 5.1 %broadcast_in_dim.11 = f32[16,640,256]{2,1,0:T(8,128)} broadcast(f32[]{:T(128)} %constant.90.clone.1), dimensions={} | broadcast | bytes 10485764 | tf_op jit(solution)/shard_map/broadcast_in_dim | solution.py:74
  120.4 31.5 %while.33 = (s32[]{:T(128)}, f32[16,640,256]{2,1,0:T(8,128)}, s32[]{:T(128)}, s32[8]{0:T(128)S(1)}, bf16[8,640,640]{2,1,0:T(8,128)(2,1)}, /*index=5*/bf16[640,25...) while((s32[]{:T(128)}, f32[16,640,256]{2,1,0:T(8,128)}, s32[]{:T(128)}, s32[8]{0:T(128)S(1)}, ...), condition=%wide.region_7.8_spmd, body=%wide.region_4.7_spmd.sunk | while | flops 209879040 | bytes 3768581 | solution.py:75
  122.7 4.2 conditional.5
  123.3 1.1 constant_dynamic-slice_fusion
  124.4 2.5 fusion.6
  129.3 4.2 conditional.5
  129.9 1.1 constant_dynamic-slice_fusion
  131.0 2.5 fusion.6
  135.8 4.2 conditional.5
  136.4 1.1 constant_dynamic-slice_fusion
  137.5 2.4 fusion.6
  151.9 7.0 %convert_element_type.44 = bf16[16,640,256]{2,1,0:T(8,128)(2,1)} convert(f32[16,640,256]{2,1,0:T(8,128)} %get-tuple-element.268) | non-fusion elementwise | flops 2621440 | bytes 15728640 | tf_op jit(solution)/shard_map/convert_element_type | solution.py:77
  159.0 214.1 %all-reduce.2.cloned.1.call-done = f32[256,256]{1,0:T(8,128)} async-done(((f32[256,256]{1,0:T(8,128)}), f32[256,256]{1,0:T(8,128)}) %all-reduce.2.cloned.1.call-update) | async-done | bytes 262160 | tf_op jit(solution)/shard_map/psum | solution.py:83
  373.1 1.7 broadcast_multiply_fusion
  374.8 94.6 %reduce-scatter.2.cloned.1.call-done = bf16[640,256]{1,0:T(8,128)(2,1)} async-done(((bf16[10240,256]{1,0:T(8,128)(2,1)}), bf16[640,256]{1,0:T(8,128)(2,1)}) %reduce-scatter.2.cloned.1.call-update) | async-done | bytes 327696 | tf_op jit(solution)/shard_map/reduce_scatter | solution.py:76
  (33 shorter events, 6.9 us)
Async XLA Ops:
  7.2 105.6 %copy-start = (bf16[256,256]{1,0:T(8,128)(2,1)S(1)}, bf16[256,256]{1,0:T(8,128)(2,1)}, u32[]{:S(2)}) copy-start(bf16[256,256]{1,0:T(8,128)(2,1)} %param.18) | copy-start | bytes 393220
  7.2 105.6 %copy-start.1 = (bf16[1,1,640,256]{3,2,1,0:T(8,128)(2,1)S(1)}, bf16[1,1,640,256]{3,2,1,0:T(8,128)(2,1)}, u32[]{:S(2)}) copy-start(bf16[1,1,640,256]{3,2,1,0:T(8,128)(2,1)} %param.19) | copy-start | bytes 983044
  7.2 72.7 %all-gather.2.cloned.1.call-start = ((), (), s32[]{:S(2)}) async-start(), calls=%async_computation.1 | async-start | bytes 5570560 | tf_op jit(solution)/shard_map/all_gather | solution.py:44
  7.9 365.2 %all-reduce.2.cloned.1.call-start = ((), (), s32[]{:S(2)}) async-start(), calls=%async_computation.3 | async-start | bytes 524288 | tf_op jit(solution)/shard_map/psum | solution.py:83
  112.7 7.7 %copy-start.2 = (s32[8]{0:T(128)S(1)}, s32[8]{0:T(128)}, u32[]{:S(2)}) copy-start(s32[8]{0:T(128)} %get-tuple-element.438) | copy-start | bytes 100
  115.0 354.4 %reduce-scatter.2.cloned.1.call-start = ((), (), s32[]{:S(2)}) async-start(), calls=%async_computation.2 | async-start | bytes 5570560 | tf_op jit(solution)/shard_map/reduce_scatter | solution.py:76
Sparse Core Ops, SparseCore 0:
  10.8 69.0 all-gather.1
  115.1 257.9 all-reduce.1
  378.1 91.2 reduce-scatter.1
where the time goes:
time: 478 us; the launch traced here: 476 us
  waiting for transfers between devices  381 us (80%)
  loops' own time  34 us (7%)
  local copies, waits for them, and re-layouts  23.1 us (5%)
  matrix products  14.8 us (3%)
  between operations  13.8 us (3%)
  other arithmetic  8.69 us (2%)
    psum x1, waiting for transfers between devices, per_device(): weight_total = lax.psum(partial_value, ('blk', 'grp'))  214 us
    reduce_scatter x1, waiting for transfers between devices, per_device(): lax.psum_scatter(totals.reshape(row_count * lax.axis_size('blk'), feat_wi...  94.6 us
    all_gather x1, waiting for transfers between devices, per_device(): lax.all_gather(features, 'blk', axis=0, tiled=True)  71.9 us
    another operation x1, loops' own time, fold_slots(): return lax.fori_loop(0, own_tiles.shape[0], fold_slot_step, running)  15.8 us
    another operation x1, loops' own time, per_device(): totals = lax.fori_loop(0, own_tiles.shape[0], adjoint_slot_step, zero_terms)  14.3 us
    dynamic_slice x8, local copies, waits for them, and re-layouts, fold_slot_step(): offset = columns[slot]  9.94 us
  transfers between devices with their start and end apart: 3, of which 3 were waited for; matrix products, arithmetic and copies ran while one was open for 6% of the time, Pallas kernels for 0%

commit v1 on v0

v1 whole, which is shorter than its diff:
```python
import functools
import math

import jax
import jax.numpy as jnp
from jax import lax
from jax.experimental import pallas as pl
from jax.experimental.pallas import tpu as pltpu
from jax.sharding import PartitionSpec as P

ROWS = 640
WIDTH = 256
SLOTS = 8
CHUNK = 128
CHUNKS = ROWS // CHUNK

ORDER = ((0, 0), (0, 3), (0, 1), (1, 0), (0, 2), (1, 2), (1, 3), (1, 1))
OWN, YM, YP, PX, Y2, PY2, PYM, PYP = range(8)


def place():
    b = lax.axis_index("blk")
    g = lax.axis_index("grp")
    return (b // 8) * 2 + g // 8, (b // 2) % 4, g % 8, b % 2


def device(x, y, z, c):
    return {"blk": (x // 2) * 8 + y * 2 + c, "grp": (x % 2) * 8 + z}


def shifted(dx=0, dy=0, dz=0, dc=0):
    x, y, z, c = place()
    return device((x + dx) % 4, (y + dy) % 4, (z + dz) % 8, (c + dc) % 2)


def gather(buf, recv, twin, sent):
    core = lax.axis_index("blk") % 2

    def rows(q):
        return pl.ds(pl.multiple_of(q * CHUNK, CHUNK), CHUNK)

    def send(src, dst, q, target):
        pltpu.make_async_remote_copy(
            buf.at[2 * src, rows(q)], buf.at[2 * dst, rows(q)], sent, recv.at[dst, q], device_id=target
        ).start()

    def pair(o, q):
        pltpu.make_async_remote_copy(
            buf.at[2 * o, rows(q)], buf.at[2 * o + 1, rows(q)], sent, twin.at[o], device_id=shifted(dc=1)
        ).start()

    def own(q):
        send(OWN, YM, q, shifted(dy=1))
        send(OWN, YP, q, shifted(dy=-1))
        send(OWN, PX, q, shifted(dx=2))
        pair(OWN, q)

    def arrived(o, q):
        pltpu.make_async_copy(buf.at[2 * o, rows(q)], buf.at[2 * o, rows(q)], recv.at[o, q]).wait()

    def first(q):
        up = (q < 2) | ((q == 2) & (core == 0))
        arrived(YM, q)

        @pl.when(up)
        def _():
            send(YM, Y2, q, shifted(dy=1))

        pair(YM, q)
        arrived(YP, q)

        @pl.when(jnp.logical_not(up))
        def _():
            send(YP, Y2, q, shifted(dy=-1))

        pair(YP, q)
        arrived(PX, q)
        send(PX, PYM, q, shifted(dy=1))
        send(PX, PYP, q, shifted(dy=-1))
        pair(PX, q)

    def second(q):
        arrived(Y2, q)
        send(Y2, PY2, q, shifted(dx=2))
        pair(Y2, q)

    def third(q):
        for o in (PY2, PYM, PYP):
            arrived(o, q)
            pair(o, q)

    def twin_arrived(o):
        pltpu.make_async_copy(buf.at[2 * o + 1], buf.at[2 * o + 1], twin.at[o]).wait()

    def drain():
        pltpu.make_async_copy(buf.at[pl.ds(0, 15)], buf.at[pl.ds(0, 15)], sent).wait()

    return own, first, second, third, twin_arrived, drain


def kernel(
    scale,
    kof,
    feat_hbm,
    tiles_hbm,
    weight_hbm,
    og_hbm,
    lo_hbm,
    fg_hbm,
    wg_hbm,
    tiles,
    g1,
    g2,
    acc,
    weight,
    og,
    agg,
    slope,
    lo,
    fg,
    wp,
    r1,
    r2,
    r3,
    r4,
    wo,
    local,
    recv1,
    twin1,
    recv2,
    twin2,
    sent,
    wrecv,
    wsent,
):
    x, y, z, c = place()
    load_f = pltpu.make_async_copy(feat_hbm, g1.at[0], local.at[0])
    load_t = pltpu.make_async_copy(tiles_hbm, tiles.at[pl.ds(0, SLOTS)], local.at[1])
    load_w = pltpu.make_async_copy(weight_hbm, weight, local.at[2])
    load_o = pltpu.make_async_copy(og_hbm, og, local.at[3])
    load_f.start()
    load_t.start()
    load_w.start()
    load_o.start()

    barrier = pltpu.get_barrier_semaphore()
    peers = [shifted(dc=1)]
    peers += [shifted(dy=d) for d in (1, 2, 3)]
    peers += [shifted(dx=d) for d in (1, 2, 3)]
    peers += [shifted(dz=d) for d in range(1, 8)]
    for peer in peers:
        pl.semaphore_signal(barrier, 1, device_id=peer)
    tiles[SLOTS] = jnp.zeros((ROWS, ROWS), jnp.bfloat16)
    load_f.wait()
    pl.semaphore_wait(barrier, len(peers))

    own, first, second, third, twin_arrived, drain1 = gather(g1, recv1, twin1, sent.at[0])
    for q in range(CHUNKS):
        own(q)

    def fold(buf, slot):
        acc[...] += jnp.dot(tiles[kof[slot]], buf[slot], preferred_element_type=jnp.float32)

    def run(buf, first, second, third, twin_arrived, hook):
        acc[...] = jnp.dot(tiles[kof[0]], buf[0], preferred_element_type=jnp.float32)

        def a_step(q, carry):
            first(q)
            hook(0, q)
            return carry

        lax.fori_loop(0, CHUNKS, a_step, 0)

        def fold_at(slot):
            @pl.when(slot % 2 == 1)
            def _():
                twin_arrived(slot // 2)

            fold(buf, slot)

        def b_step(q, carry):
            second(q)
            hook(1, q)
            fold_at(1 + q)
            return carry

        lax.fori_loop(0, CHUNKS, b_step, 0)

        def c_step(q, carry):
            third(q)
            hook(2, q)
            fold_at(6 + q)
            return carry

        lax.fori_loop(0, CHUNKS, c_step, 0)

        def d_step(s, carry):
            fold_at(s)
            return carry

        lax.fori_loop(11, 16, d_step, 0)

    load_t.wait()
    run(g1, first, second, third, twin_arrived, lambda phase, q: None)
    load_w.wait()
    load_o.wait()

    own, first, second, third, twin_arrived, drain2 = gather(g2, recv2, twin2, sent.at[1])

    def middle(q, carry):
        rows = pl.ds(pl.multiple_of(q * CHUNK, CHUNK), CHUNK)
        a = acc[rows, :].astype(jnp.bfloat16)
        agg[rows, :] = a
        linear = jnp.dot(a, weight[...], preferred_element_type=jnp.float32)
        sig = jax.nn.sigmoid(linear)
        lo[rows, :] = (linear * sig).astype(jnp.bfloat16)
        s = (og[rows, :].astype(jnp.float32) * (sig * (1.0 + linear * (1.0 - sig)))).astype(jnp.bfloat16)
        slope[rows, :] = s
        g2[0, rows, :] = lax.dot_general(
            s, weight[...], (((1,), (1,)), ((), ())), preferred_element_type=jnp.float32
        ).astype(jnp.bfloat16)
        own(q)
        return carry

    lax.fori_loop(0, CHUNKS, middle, 0)
    store_lo = pltpu.make_async_copy(lo, lo_hbm, local.at[4])
    store_lo.start()
    partial = lax.dot_general(
        agg[...], slope[...], (((0,), (0,)), ((), ())), preferred_element_type=jnp.float32
    )
    wp[...] = partial.reshape(wp.shape)

    def stage(i, ref, n):
        return wrecv.at[i], wsent.at[i]

    def put(i, src, dst, target):
        pltpu.make_async_remote_copy(src, dst, wsent.at[i], wrecv.at[i], device_id=target).start()

    def got(i, ref):
        pltpu.make_async_copy(ref, ref, wrecv.at[i]).wait()

    put(0, wp.at[1 - c], r1, shifted(dc=1))

    def over_z():
        got(0, r1)
        wp[c] = wp[c] + r1[...]
        for d in range(1, 8):
            put(1, wp.at[c, (z + d) % 8], r2.at[d - 1], shifted(dz=d))

    def over_x():
        got(1, r2)
        r3[x] = wp[c, z] + jnp.sum(r2[...], axis=0)
        for d in range(1, 4):
            put(2, r3.at[x], r3.at[x], shifted(dx=d))

    def over_y():
        got(2, r3.at[pl.ds(0, 3)])
        r4[y] = (r3[0] + r3[1]) + (r3[2] + r3[3])
        for d in range(1, 4):
            put(3, r4.at[y], r4.at[y], shifted(dy=d))

    def back_z():
        got(3, r4.at[pl.ds(0, 3)])
        wo[c, z] = ((r4[0] + r4[1]) + (r4[2] + r4[3])) * scale
        for d in range(1, 8):
            put(4, wo.at[c, z], wo.at[c, z], shifted(dz=d))

    def back_core():
        got(4, r2)
        put(5, wo.at[c], wo.at[c], shifted(dc=1))

    hooks = {(0, 1): over_z, (0, 4): over_x, (1, 2): over_y, (1, 4): back_z, (2, 2): back_core}

    def hook(phase, q):
        for (ph, at), f in hooks.items():
            if ph == phase:
                pl.when(q == at)(f)

    run(g2, first, second, third, twin_arrived, hook)
    fg[...] = acc[...].astype(jnp.bfloat16)
    store_fg = pltpu.make_async_copy(fg, fg_hbm, local.at[5])
    store_fg.start()
    got(5, wo.at[1 - c])
    store_wg = pltpu.make_async_copy(wo, wg_hbm, local.at[6])
    store_wg.start()

    drain1()
    drain2()
    for i, ref in enumerate((r1, r2, r3.at[pl.ds(0, 3)], r4.at[pl.ds(0, 3)], r2, wo.at[0])):
        pltpu.make_async_copy(ref, ref, wsent.at[i]).wait()
    store_lo.wait()
    store_fg.wait()
    store_wg.wait()


def per_device(features, tiles, slot_columns, slot_counts, weight, out_grad):
    b = lax.axis_index("blk")
    p, y, c = b // 8, (b // 2) % 4, b % 2
    columns = slot_columns[0, 0]
    count = slot_counts[0, 0]
    blocks = jnp.stack(
        [
            ((p + dp) % 2) * 8 + ((y + dy) % 4) * 2 + (c + dc) % 2
            for dp, dy in ORDER
            for dc in range(2)
        ]
    )
    slots = jnp.arange(SLOTS, dtype=jnp.int32)
    match = (columns[None, :] == blocks[:, None]) & (slots[None, :] < count)
    kof = jnp.min(jnp.where(match, slots[None, :], SLOTS), axis=1).astype(jnp.int32)
    scale = 1.0 / math.sqrt(ROWS * 256)
    bf, f32 = jnp.bfloat16, jnp.float32
    any_spec = pl.BlockSpec(memory_space=pl.ANY)
    dma = pltpu.SemaphoreType.DMA
    lo, fg, wg = pl.pallas_call(
        functools.partial(kernel, scale),
        name="graph_layer",
        out_shape=(
            jax.ShapeDtypeStruct((ROWS, WIDTH), bf),
            jax.ShapeDtypeStruct((ROWS, WIDTH), bf),
            jax.ShapeDtypeStruct((2, 8, 16, WIDTH), f32),
        ),
        in_specs=[pl.BlockSpec(memory_space=pltpu.SMEM)] + [any_spec] * 4,
        out_specs=(any_spec, any_spec, any_spec),
        scratch_shapes=[
            pltpu.VMEM((SLOTS + 1, ROWS, ROWS), bf),
            pltpu.VMEM((16, ROWS, WIDTH), bf),
            pltpu.VMEM((16, ROWS, WIDTH), bf),
            pltpu.VMEM((ROWS, WIDTH), f32),
            pltpu.VMEM((WIDTH, WIDTH), bf),
            pltpu.VMEM((ROWS, WIDTH), bf),
            pltpu.VMEM((ROWS, WIDTH), bf),
            pltpu.VMEM((ROWS, WIDTH), bf),
            pltpu.VMEM((ROWS, WIDTH), bf),
            pltpu.VMEM((ROWS, WIDTH), bf),
            pltpu.VMEM((2, 8, 16, WIDTH), f32),
            pltpu.VMEM((8, 16, WIDTH), f32),
            pltpu.VMEM((7, 16, WIDTH), f32),
            pltpu.VMEM((4, 16, WIDTH), f32),
            pltpu.VMEM((4, 16, WIDTH), f32),
            pltpu.VMEM((2, 8, 16, WIDTH), f32),
            dma((7,)),
            dma((8, CHUNKS)),
            dma((8,)),
            dma((8, CHUNKS)),
            dma((8,)),
            dma((2,)),
            dma((6,)),
            dma((6,)),
        ],
        compiler_params=pltpu.CompilerParams(
            collective_id=0, has_side_effects=True, vmem_limit_bytes=48 << 20
        ),
    )(kof, features[0, 0], tiles[0, 0], weight, out_grad[0, 0])
    return lo[None, None], fg[None, None], wg.reshape(WIDTH, WIDTH)


def solution(mesh):
    in_specs = (
        P("blk", "grp", None, None),
        P("blk", "grp", None, None, None),
        P("blk", "grp", None),
        P("blk", "grp"),
        P(),
        P("blk", "grp", None, None),
    )
    out_specs = (P("blk", "grp", None, None), P("blk", "grp", None, None), P())
    return jax.shard_map(
        per_device, mesh=mesh, in_specs=in_specs, out_specs=out_specs, check_vma=False
    )
```

time: 478 us -> 76.4 us (0.16)
  waiting for transfers between devices: 381 us -> 0 us
  Pallas kernels: 0 us -> 68.8 us
  loops' own time: 34 us -> 0 us
  local copies, waits for them, and re-layouts: 23.1 us -> 5.09 us
  matrix products: 14.8 us -> 0 us
  between operations: 13.8 us -> 1.47 us
  other arithmetic: 8.69 us -> 0.75 us
    psum x1 -> x0, waiting for transfers between devices: 214 us -> none  [per_device(): weight_total = lax.psum(partial_value, ('blk', 'grp'))]
    reduce_scatter x1 -> x0, waiting for transfers between devices: 94.6 us -> none  [per_device(): lax.psum_scatter(totals.reshape(row_count * lax.axis_size('blk'), feat_wi...]
    all_gather x1 -> x0, waiting for transfers between devices: 71.9 us -> none  [per_device(): lax.all_gather(features, 'blk', axis=0, tiled=True)]
    pallas_call x0 -> x1, Pallas kernels: none -> 68.8 us  [per_device(): pl.pallas_call(functools.partial(kernel, scale), name='graph_layer', out_...]
    another operation x18 -> x0, loops' own time: 34 us -> none  [the longest x1 15.8 us: fold_slots(): return lax.fori_loop(0, own_tiles.shape[0], fold_slot_step, running)]
    dynamic_slice x19 -> x0, local copies, waits for them, and re-layouts: 18 us -> none  [the longest x8 9.94 us: fold_slot_step(): offset = columns[slot]]
    dot_general x9 -> x0, matrix products: 14.8 us -> none  [the longest x3 7.38 us: adjoint_accumulate(): lax.dot_general(own_tiles[slot], panel_grad, (((0,), (0,)), ((), ())), pr...]
    convert_element_type x1 -> x0, other arithmetic: 7.02 us -> none  [per_device(): totals.reshape(row_count * lax.axis_size('blk'), feat_width)]
  transfers between devices with their start and end apart: 3 -> 0, of which waited for: 3 -> 0; matrix products, arithmetic and copies ran while one was open for 6% -> 0% of each run, Pallas kernels for 0% -> 0%
where the time goes in v1:
time: 76.4 us; the launch traced here: 76.2 us
  Pallas kernels  68.8 us (90%)
  local copies, waits for them, and re-layouts  5.09 us (7%)
  between operations  1.47 us (2%)
    pallas_call x1, Pallas kernels, per_device(): pl.pallas_call(functools.partial(kernel, scale), name='graph_layer', out_...  68.8 us
    unnamed x9, local copies, waits for them, and re-layouts  4.99 us

profile of v1, /device:TPU:1, one launch (start us, length us, event | category | flops | bytes accessed | tf_op | source)
XLA Modules:
  0.0 76.2 jit_solution(438450080133082323)
XLA Ops:
  1.4 0.1 stack.67
  1.6 0.7 select_reduce_fusion.kof
  2.3 0.0 copy-start
  2.3 1.0 %copy-done = bf16[1,1,640,256]{3,2,1,0:T(8,128)(2,1)S(1)} copy-done((bf16[1,1,640,256]{3,2,1,0:T(8,128)(2,1)S(1)}, bf16[1,1,640,256]{3,2,1,0:T(8,128)(2,1)}, u32[]{:S(2)}) %copy-start) | copy-done | bytes 327704
  3.3 0.0 copy-start.1
  3.3 1.0 %copy-done.1 = bf16[1,1,640,256]{3,2,1,0:T(8,128)(2,1)S(1)} copy-done((bf16[1,1,640,256]{3,2,1,0:T(8,128)(2,1)S(1)}, bf16[1,1,640,256]{3,2,1,0:T(8,128)(2,1)}, u32[]{:S(2)}) %copy-start.1) | copy-done | bytes 327704
  4.2 0.0 copy-start.2
  4.2 0.9 %copy-done.2 = bf16[256,256]{1,0:T(8,128)(2,1)S(1)} copy-done((bf16[256,256]{1,0:T(8,128)(2,1)S(1)}, bf16[256,256]{1,0:T(8,128)(2,1)}, u32[]{:S(2)}) %copy-start.2) | copy-done | bytes 131096
  5.1 68.8 %graph_layer.1 = (bf16[640,256]{1,0:T(8,128)(2,1)S(1)}, bf16[640,256]{1,0:T(8,128)(2,1)S(1)}, f32[2,8,16,256]{3,2,1,0:T(8,128)S(1)}) custom-call(s32[16]{0:T(128)S(1)} %select_reduce_fusion.kof, bf16[640,256]{1,0:T(8,128)(2,1)S(1)} %bitcast.27, bf16[8,640,640]{2,1,0:T(8,128)(2,1)} %bitcast.30, bf16[256,256]{1,0:T(8,128)(2,1)S(1)} %copy-done.2, ...), custom_call_target="tpu_custom_call" | custom-call | tf_op jit(solution)/shard_map/graph_layer/pallas_call | solution.py:315
  74.0 0.7 copy.13
  74.7 0.7 copy.14
  75.5 0.7 copy.15
  (1 shorter events, 0.0 us)
Async XLA Ops:
  2.3 1.0 %copy-start = (bf16[1,1,640,256]{3,2,1,0:T(8,128)(2,1)S(1)}, bf16[1,1,640,256]{3,2,1,0:T(8,128)(2,1)}, u32[]{:S(2)}) copy-start(bf16[1,1,640,256]{3,2,1,0:T(8,128)(2,1)} %param.6) | copy-start | bytes 983044
  3.3 1.0 %copy-start.1 = (bf16[1,1,640,256]{3,2,1,0:T(8,128)(2,1)S(1)}, bf16[1,1,640,256]{3,2,1,0:T(8,128)(2,1)}, u32[]{:S(2)}) copy-start(bf16[1,1,640,256]{3,2,1,0:T(8,128)(2,1)} %param.11) | copy-start | bytes 983044
  4.2 0.9 %copy-start.2 = (bf16[256,256]{1,0:T(8,128)(2,1)S(1)}, bf16[256,256]{1,0:T(8,128)(2,1)}, u32[]{:S(2)}) copy-start(bf16[256,256]{1,0:T(8,128)(2,1)} %weight_hbm.1) | copy-start | bytes 393220

commit v2 on v1

v2 whole, which is shorter than its diff:
```python
import functools
import math

import jax
import jax.numpy as jnp
from jax import lax
from jax.experimental import pallas as pl
from jax.experimental.pallas import tpu as pltpu
from jax.sharding import PartitionSpec as P

ROWS = 640
WIDTH = 256
SLOTS = 8
CHUNK = 128
CHUNKS = ROWS // CHUNK
MADE = (0, 4, 1, 3, 2)

ORDER = ((0, 0), (0, 3), (0, 1), (1, 0), (0, 2), (1, 2), (1, 3), (1, 1))
OWN, YM, YP, PX, Y2, PY2, PYM, PYP = range(8)


def place():
    b = lax.axis_index("blk")
    g = lax.axis_index("grp")
    return (b // 8) * 2 + g // 8, (b // 2) % 4, g % 8, b % 2


def device(x, y, z, c):
    return {"blk": (x // 2) * 8 + y * 2 + c, "grp": (x % 2) * 8 + z}


def shifted(dx=0, dy=0, dz=0, dc=0):
    x, y, z, c = place()
    return device((x + dx) % 4, (y + dy) % 4, (z + dz) % 8, (c + dc) % 2)


class Gather:
    def __init__(self, buf, recv, twin, sent):
        self.buf, self.recv, self.twin, self.sent = buf, recv, twin, sent
        self.core = lax.axis_index("blk") % 2

    def send(self, src, dst, q, at, **shift):
        rows = pl.ds(q * CHUNK, CHUNK)
        pltpu.make_async_remote_copy(
            self.buf.at[2 * src, rows],
            self.buf.at[2 * dst, rows],
            self.sent,
            self.recv.at[at],
            device_id=shifted(**shift),
        ).start()

    def pair(self, o, at, *chunks):
        for q in chunks:
            rows = pl.ds(q * CHUNK, CHUNK)
            pltpu.make_async_remote_copy(
                self.buf.at[2 * o, rows],
                self.buf.at[2 * o + 1, rows],
                self.sent,
                self.twin.at[at],
                device_id=shifted(dc=1),
            ).start()

    def wait(self, sem, chunks):
        if chunks <= CHUNKS:
            ref = self.buf.at[0, pl.ds(0, CHUNK * chunks)]
        elif chunks % CHUNKS == 0:
            ref = self.buf.at[pl.ds(0, chunks // CHUNKS)]
        else:
            ref = self.buf.at[pl.ds(0, chunks // 2), pl.ds(0, 2 * CHUNK)]
        pltpu.make_async_copy(ref, ref, sem).wait()

    def got(self, at):
        self.wait(self.recv.at[at], (2, 2, 2, 4, 2, 3, 2, 2, 1, 2, 2, 1, 4, 4, 2)[at])

    def got_twin(self, at):
        self.wait(self.twin.at[at], (5, 4, 6, 2, 3, 5, 4, 1, 4, 4, 2)[at])

    def own(self, step):
        ups, downs = (((0,), ()), ((), (4,)), ((1,), ()), ((), (3,)), ((2, 3, 4), (2, 1, 0)))[step]
        for i in range(3):
            if i < len(ups):
                q = ups[i]
                self.send(OWN, YM, q, min(q, 3), dy=1)
                self.send(OWN, PX, q, 4 if q < 2 else 5, dx=2)
            if i < len(downs):
                q = downs[i]
                self.send(OWN, YP, q, min(4 - q, 3), dy=-1)
        self.pair(OWN, 0, MADE[step])

    def sides(self, i):
        self.got(i)
        if i < 2:
            self.send(YM, Y2, i, 6 + i, dy=1)
            self.send(YP, Y2, 4 - i, 6 + i, dy=-1)
        if i == 0:
            self.send(YM, PYM, 0, 12, dx=2)
            self.send(YP, PYP, 4, 12, dx=2)
        if i == 2:
            pl.when(self.core == 0)(lambda: self.send(YM, Y2, 2, 8, dy=1))
            pl.when(self.core == 1)(lambda: self.send(YP, Y2, 2, 8, dy=-1))
        part = 1 if i < 2 else 2
        ups = (i,) if i < 3 else (3, 4)
        self.pair(YM, part, *ups)
        self.pair(YP, part, *(4 - q for q in ups))

    def across(self, i):
        self.got(4 + i)
        self.pair(PX, 3 + i, *((0, 1), (2, 3, 4))[i])

    def across_on(self, i):
        self.send(PX, PYM, 1 + i, 12 + (1 + i) // 2, dy=1)
        self.send(PX, PYP, 3 - i, 12 + (1 + i) // 2, dy=-1)

    def opposite(self, i):
        self.got(6 + i)
        for q in ((0, 4), (1, 3), (2,))[i]:
            self.send(Y2, PY2, q, 9 + i, dx=2)
            self.pair(Y2, 5, q)

    def far_opposite(self, i):
        self.got(9 + i)
        self.pair(PY2, 6 if i < 2 else 7, *((0, 4), (1, 3), (2,))[i])

    def far_sides(self, i):
        self.got(12 + i)
        self.pair(PYM, 8 + i, *((0, 1), (2, 3), (4,))[i])
        self.pair(PYP, 8 + i, *((4, 3), (2, 1), (0,))[i])

    def drain(self):
        self.wait(self.sent, 75)


def run(net, tiles, kof, acc, hooks):
    buf = net.buf
    hooked = bool(hooks)

    def hook(at):
        if hooked:
            hooks[at]()

    def fold(slot, begin=0, end=CHUNKS):
        span = pl.ds(CHUNK * begin, CHUNK * (end - begin))
        acc[...] += jnp.dot(tiles[kof[slot], :, span], buf[slot, span], preferred_element_type=jnp.float32)

    def fold_twins(o, begin, end):
        def step(slot, carry):
            fold(slot, begin, end)
            return carry

        lax.fori_loop(2 * o, 2 * o + 2, step, 0)

    acc[...] = jnp.dot(tiles[kof[0]], buf[0], preferred_element_type=jnp.float32)
    net.sides(0)
    hook(0)
    net.got_twin(0)
    fold(1)
    net.sides(1)
    fold(2 * YM, 0, 2)
    fold(2 * YP, 3, 5)
    net.sides(2)
    net.across(0)
    net.got_twin(1)
    fold(2 * YM + 1, 0, 2)
    fold(2 * YP + 1, 3, 5)
    net.got_twin(3)
    fold_twins(PX, 0, 2)
    hook(1)
    net.sides(3)
    net.across(1)
    net.across_on(0)
    if not hooked:
        for i in range(1, 4):
            net.across_on(i)
    fold(2 * YM, 2, 5)
    net.opposite(0)
    net.got_twin(2)
    fold(2 * YM + 1, 2, 5)
    fold(2 * YP, 0, 3)
    if hooked:
        hook(2)
        for i in range(1, 4):
            net.across_on(i)
    net.opposite(1)
    fold(2 * YP + 1, 0, 3)
    net.opposite(2)
    net.got_twin(4)
    fold_twins(PX, 2, 5)
    fold(2 * Y2)
    net.far_sides(0)
    net.got_twin(5)
    fold(2 * Y2 + 1)
    net.far_opposite(0)
    hook(3)
    fold(2 * PYM, 0, 2)
    fold(2 * PYP, 3, 5)
    net.got_twin(8)
    fold(2 * PYM + 1, 0, 2)
    fold(2 * PYP + 1, 3, 5)
    net.far_sides(1)
    fold(2 * PYM, 2, 4)
    fold(2 * PYP, 1, 3)
    net.far_opposite(1)
    net.got_twin(9)
    fold(2 * PYM + 1, 2, 4)
    fold(2 * PYP + 1, 1, 3)
    net.far_sides(2)
    fold(2 * PY2, 0, 2)
    net.far_opposite(2)
    hook(4)
    fold(2 * PY2, 3, 5)
    net.got_twin(6)
    fold(2 * PY2 + 1, 0, 2)
    fold(2 * PY2 + 1, 3, 5)

    spans = [(o, pl.ds(q * CHUNK, CHUNK)) for o, q in ((PYM, 4), (PYP, 0), (PY2, 2))]

    def rest(rows, dc):
        a = jnp.concatenate([tiles[kof[2 * o + dc], rows, span] for o, span in spans], axis=1)
        v = jnp.concatenate([buf[2 * o + dc, span] for o, span in spans], axis=0)
        return jnp.dot(a, v, preferred_element_type=jnp.float32)

    acc[...] += rest(pl.ds(0, ROWS), 0)
    net.got_twin(7)
    net.got_twin(10)
    return lambda rows: acc[rows, :] + rest(rows, 1)


def kernel(
    scale,
    columns,
    count,
    feat_hbm,
    tiles_hbm,
    weight_hbm,
    og_hbm,
    lo_hbm,
    fg_hbm,
    wg_hbm,
    kof,
    tiles,
    g1,
    g2,
    acc,
    weight,
    og,
    agg,
    slope,
    lo,
    fg,
    wp,
    wb,
    r1,
    r2,
    r3,
    r4,
    wo,
    local,
    recv1,
    twin1,
    recv2,
    twin2,
    sent,
    wrecv,
    wsent,
):
    x, y, z, c = place()
    load_f = pltpu.make_async_copy(feat_hbm, g1.at[0], local.at[0])
    load_t = pltpu.make_async_copy(tiles_hbm, tiles.at[pl.ds(0, SLOTS)], local.at[1])
    load_w = pltpu.make_async_copy(weight_hbm, weight, local.at[2])
    load_o = pltpu.make_async_copy(og_hbm, og, local.at[2])
    load_f.start()
    barrier = pltpu.get_barrier_semaphore()
    peers = [shifted(dc=1)]
    peers += [shifted(dy=d) for d in (1, 2, 3)]
    peers += [shifted(dx=d) for d in (1, 2, 3)]
    peers += [shifted(dz=d) for d in range(1, 8)]
    for peer in peers:
        pl.semaphore_signal(barrier, 1, device_id=peer)
    load_t.start()
    load_w.start()
    load_o.start()
    pl.semaphore_wait(barrier, len(peers))
    load_f.wait()

    net1 = Gather(g1, recv1, twin1, sent.at[0])
    for step in range(CHUNKS):
        net1.own(step)
    tiles[SLOTS] = jnp.zeros((ROWS, ROWS), jnp.bfloat16)
    for o, (dp, dy) in enumerate(ORDER):
        for dc in range(2):
            block = ((x // 2 + dp) % 2) * 8 + ((y + dy) % 4) * 2 + (c + dc) % 2
            slot = jnp.int32(SLOTS)
            for k in range(SLOTS - 1, -1, -1):
                slot = jnp.where((columns[k] == block) & (k < count[0]), k, slot)
            kof[2 * o + dc] = slot
    load_t.wait()
    total = run(net1, tiles, kof, acc, ())
    pltpu.make_async_copy(acc.at[pl.ds(0, 448)], acc.at[pl.ds(0, 448)], local.at[2]).wait()

    net2 = Gather(g2, recv2, twin2, sent.at[1])
    for step in range(CHUNKS):
        rows = pl.ds(MADE[step] * CHUNK, CHUNK)
        a = total(rows).astype(jnp.bfloat16)
        agg[rows, :] = a
        linear = jnp.dot(a, weight[...], preferred_element_type=jnp.float32)
        sig = jax.nn.sigmoid(linear)
        lo[rows, :] = (linear * sig).astype(jnp.bfloat16)
        s = (og[rows, :].astype(jnp.float32) * (sig * (1.0 + linear * (1.0 - sig)))).astype(jnp.bfloat16)
        slope[rows, :] = s
        g2[0, rows, :] = lax.dot_general(
            s, weight[...], (((1,), (1,)), ((), ())), preferred_element_type=jnp.float32
        ).astype(jnp.bfloat16)
        net2.own(step)

    store_lo = pltpu.make_async_copy(lo, lo_hbm, local.at[0])
    store_lo.start()
    partial = lax.dot_general(
        agg[...], slope[...], (((0,), (0,)), ((), ())), preferred_element_type=jnp.float32
    )
    wp[...] = partial.reshape(wp.shape)

    def put(i, src, dst, target):
        pltpu.make_async_remote_copy(src, dst, wsent.at[0], wrecv.at[i], device_id=target).start()

    def got(i, ref):
        pltpu.make_async_copy(ref, ref, wrecv.at[i]).wait()

    put(0, wp.at[1 - c], r1, shifted(dc=1))

    def over_z():
        got(0, r1)
        wb[...] = (wp[c] + r1[...]).astype(jnp.bfloat16)
        for d in range(1, 8):
            put(1, wb.at[(z + d) % 8], r2.at[d - 1], shifted(dz=d))

    def over_x():
        got(1, r2)
        total = wb[z].astype(jnp.float32) + jnp.sum(r2[...].astype(jnp.float32), axis=0)
        r3[x] = total.astype(jnp.bfloat16)
        for d in range(1, 4):
            put(2, r3.at[x], r3.at[x], shifted(dx=d))

    def four(ref):
        v = ref[...].astype(jnp.float32)
        return (v[0] + v[1]) + (v[2] + v[3])

    def over_y():
        got(2, r3.at[pl.ds(0, 3)])
        r4[y] = four(r3).astype(jnp.bfloat16)
        for d in range(1, 4):
            put(3, r4.at[y], r4.at[y], shifted(dy=d))

    def back_z():
        got(3, r4.at[pl.ds(0, 3)])
        wo[c, z] = (four(r4) * scale).astype(jnp.bfloat16)
        for d in range(1, 8):
            put(4, wo.at[c, z], wo.at[c, z], shifted(dz=d))

    def back_core():
        got(4, r2)
        put(5, wo.at[c], wo.at[c], shifted(dc=1))

    hooks = (over_z, over_x, over_y, back_z, back_core)
    total = run(net2, tiles, kof, acc, hooks)
    for q in range(CHUNKS):
        rows = pl.ds(q * CHUNK, CHUNK)
        fg[rows, :] = total(rows).astype(jnp.bfloat16)
        pltpu.make_async_copy(fg.at[rows], fg_hbm.at[rows], local.at[1]).start()
    got(5, wo.at[1 - c])
    store_wg = pltpu.make_async_copy(wo, wg_hbm, local.at[2])
    store_wg.start()

    net1.drain()
    net2.drain()
    pltpu.make_async_copy(acc.at[pl.ds(0, 352)], acc.at[pl.ds(0, 352)], wsent.at[0]).wait()
    store_lo.wait()
    pltpu.make_async_copy(fg, fg_hbm, local.at[1]).wait()
    store_wg.wait()


def hand_out(lo, fg, wg, lo_out, fg_out, wg_out, blocks, wide, narrow, sems):
    def copy(src, dst, i):
        made = pltpu.make_async_copy(src, dst, sems.at[i])
        made.start()
        return made

    came = [copy(wg, narrow, 0), copy(lo, blocks.at[0], 1), copy(fg, blocks.at[1], 2)]
    came[0].wait()
    wide[...] = narrow[...].astype(jnp.float32)
    gone = [copy(wide, wg_out, 3)]
    came[1].wait()
    gone.append(copy(blocks.at[0], lo_out, 4))
    came[2].wait()
    gone.append(copy(blocks.at[1], fg_out, 5))
    for made in gone:
        made.wait()


def per_device(features, tiles, slot_columns, slot_counts, weight, out_grad):
    scale = 1.0 / math.sqrt(ROWS * 256)
    bf, f32 = jnp.bfloat16, jnp.float32
    any_spec = pl.BlockSpec(memory_space=pl.ANY)
    dma = pltpu.SemaphoreType.DMA
    lo, fg, wg = pl.pallas_call(
        functools.partial(kernel, scale),
        name="graph_layer",
        out_shape=(
            jax.ShapeDtypeStruct((ROWS, WIDTH), bf),
            jax.ShapeDtypeStruct((ROWS, WIDTH), bf),
            jax.ShapeDtypeStruct((2, 8, 16, WIDTH), bf),
        ),
        in_specs=[pl.BlockSpec(memory_space=pltpu.SMEM)] * 2 + [any_spec] * 4,
        out_specs=(any_spec, any_spec, any_spec),
        scratch_shapes=[
            pltpu.SMEM((16,), jnp.int32),
            pltpu.VMEM((SLOTS + 1, ROWS, ROWS), bf),
            pltpu.VMEM((16, ROWS, WIDTH), bf),
            pltpu.VMEM((16, ROWS, WIDTH), bf),
            pltpu.VMEM((ROWS, WIDTH), f32),
            pltpu.VMEM((WIDTH, WIDTH), bf),
            pltpu.VMEM((ROWS, WIDTH), bf),
            pltpu.VMEM((ROWS, WIDTH), bf),
            pltpu.VMEM((ROWS, WIDTH), bf),
            pltpu.VMEM((ROWS, WIDTH), bf),
            pltpu.VMEM((ROWS, WIDTH), bf),
            pltpu.VMEM((2, 8, 16, WIDTH), f32),
            pltpu.VMEM((8, 16, WIDTH), bf),
            pltpu.VMEM((8, 16, WIDTH), f32),
            pltpu.VMEM((7, 16, WIDTH), bf),
            pltpu.VMEM((4, 16, WIDTH), bf),
            pltpu.VMEM((4, 16, WIDTH), bf),
            pltpu.VMEM((2, 8, 16, WIDTH), bf),
            dma((3,)),
            dma((15,)),
            dma((11,)),
            dma((15,)),
            dma((11,)),
            dma((2,)),
            dma((6,)),
            dma((1,)),
        ],
        compiler_params=pltpu.CompilerParams(
            collective_id=0, has_side_effects=True, vmem_limit_bytes=62 << 20
        ),
    )(slot_columns[0, 0], slot_counts[0], features[0, 0], tiles[0, 0], weight, out_grad[0, 0])
    lo, fg, wg = pl.pallas_call(
        hand_out,
        name="hand_out",
        out_shape=(
            jax.ShapeDtypeStruct((ROWS, WIDTH), bf),
            jax.ShapeDtypeStruct((ROWS, WIDTH), bf),
            jax.ShapeDtypeStruct((WIDTH, WIDTH), f32),
        ),
        in_specs=[any_spec] * 3,
        out_specs=(any_spec,) * 3,
        scratch_shapes=[pltpu.VMEM((2, ROWS, WIDTH), bf), pltpu.VMEM((WIDTH, WIDTH), f32), pltpu.VMEM((WIDTH, WIDTH), bf), dma((6,))],
    )(lo, fg, wg.reshape(WIDTH, WIDTH))
    return lo[None, None], fg[None, None], wg


def solution(mesh):
    in_specs = (
        P("blk", "grp", None, None),
        P("blk", "grp", None, None, None),
        P("blk", "grp", None),
        P("blk", "grp"),
        P(),
        P("blk", "grp", None, None),
    )
    out_specs = (P("blk", "grp", None, None), P("blk", "grp", None, None), P())
    return jax.shard_map(
        per_device, mesh=mesh, in_specs=in_specs, out_specs=out_specs, check_vma=False
    )
```

time: 76.4 us -> 60.4 us (0.79)
  Pallas kernels: 68.8 us -> 59 us
  local copies, waits for them, and re-layouts: 5.09 us -> 0 us
    pallas_call x1, Pallas kernels: 68.8 us -> 57.1 us  [per_device(): pl.pallas_call(functools.partial(kernel, scale), name='graph_layer', out_...]
    unnamed x9 -> x0, local copies, waits for them, and re-layouts: 4.99 us -> none
    pallas_call x0 -> x1, Pallas kernels: none -> 1.93 us  [per_device(): pl.pallas_call(hand_out, name='hand_out', out_shape=(jax.ShapeDtypeStruct...]
where the time goes in v2:
time: 60.4 us; the launch traced here: 60.3 us
  Pallas kernels  59 us (98%)
  between operations  1.29 us (2%)
    pallas_call x1, Pallas kernels, per_device(): pl.pallas_call(functools.partial(kernel, scale), name='graph_layer', out_...  57.1 us
    pallas_call x1, Pallas kernels, per_device(): pl.pallas_call(hand_out, name='hand_out', out_shape=(jax.ShapeDtypeStruct...  1.93 us

profile of v2, /device:TPU:1, one launch (start us, length us, event | category | flops | bytes accessed | tf_op | source)
XLA Modules:
  0.0 60.3 jit_solution(474326594292679875)
XLA Ops:
  1.3 57.1 %graph_layer.1 = (bf16[640,256]{1,0:T(8,128)(2,1)}, bf16[640,256]{1,0:T(8,128)(2,1)}, bf16[2,8,16,256]{3,2,1,0:T(8,128)(2,1)}) custom-call(s32[8]{0:T(128)} %bitcast.13, s32[1]{0:T(128)} %bitcast.8.count, bf16[640,256]{1,0:T(8,128)(2,1)} %bitcast.10, bf16[8,640,640]{2,1,0:T(8,128)(2,1)} %bitcast.9, bf16[256,256]{1,0:T(8,128)(2,1)} %weight_hbm.1, ...), custom_call_target="tpu_custom_call" | custom-call | tf_op jit(solution)/shard_map/graph_layer/pallas_call | solution.py:404
  58.4 1.9 %hand_out.1 = (bf16[640,256]{1,0:T(8,128)(2,1)}, bf16[640,256]{1,0:T(8,128)(2,1)}, f32[256,256]{1,0:T(8,128)}) custom-call(bf16[640,256]{1,0:T(8,128)(2,1)} %get-tuple-element.9.lo, bf16[640,256]{1,0:T(8,128)(2,1)} %get-tuple-element.10.fg, bf16[256,256]{1,0:T(8,128)(2,1)} %bitcast.12), custom_call_target="tpu_custom_call" | custom-call | tf_op jit(solution)/shard_map/hand_out/pallas_call | solution.py:446

commit v3 on v2

--- a/solution.py
+++ b/solution.py
@@ -92,9 +92,6 @@
         if i < 2:
             self.send(YM, Y2, i, 6 + i, dy=1)
             self.send(YP, Y2, 4 - i, 6 + i, dy=-1)
-        if i == 0:
-            self.send(YM, PYM, 0, 12, dx=2)
-            self.send(YP, PYP, 4, 12, dx=2)
         if i == 2:
             pl.when(self.core == 0)(lambda: self.send(YM, Y2, 2, 8, dy=1))
             pl.when(self.core == 1)(lambda: self.send(YP, Y2, 2, 8, dy=-1))
@@ -103,6 +100,9 @@
         self.pair(YM, part, *ups)
         self.pair(YP, part, *(4 - q for q in ups))
 
+    def early(self, i):
+        self.send((YM, YP)[i], (PYM, PYP)[i], (0, 4)[i], 12, dx=2)
+
     def across(self, i):
         self.got(4 + i)
         self.pair(PX, 3 + i, *((0, 1), (2, 3, 4))[i])
@@ -151,6 +151,8 @@
 
     acc[...] = jnp.dot(tiles[kof[0]], buf[0], preferred_element_type=jnp.float32)
     net.sides(0)
+    net.early(0)
+    net.early(1)
     hook(0)
     net.got_twin(0)
     fold(1)
@@ -162,25 +164,36 @@
     net.got_twin(1)
     fold(2 * YM + 1, 0, 2)
     fold(2 * YP + 1, 3, 5)
-    net.got_twin(3)
-    fold_twins(PX, 0, 2)
-    hook(1)
-    net.sides(3)
-    net.across(1)
-    net.across_on(0)
-    if not hooked:
-        for i in range(1, 4):
-            net.across_on(i)
-    fold(2 * YM, 2, 5)
-    net.opposite(0)
-    net.got_twin(2)
-    fold(2 * YM + 1, 2, 5)
-    fold(2 * YP, 0, 3)
     if hooked:
+        net.got_twin(3)
+        fold_twins(PX, 0, 2)
+        hook(1)
+        net.sides(3)
+        net.across(1)
+        net.across_on(0)
+        fold(2 * YM, 2, 5)
+        net.opposite(0)
+        net.got_twin(2)
+        fold(2 * YM + 1, 2, 5)
+        fold(2 * YP, 0, 3)
         hook(2)
         for i in range(1, 4):
             net.across_on(i)
-    net.opposite(1)
+        net.opposite(1)
+    else:
+        fold(2 * PX, 0, 2)
+        net.sides(3)
+        net.across(1)
+        for i in range(4):
+            net.across_on(i)
+        net.opposite(0)
+        net.got_twin(3)
+        fold(2 * PX + 1, 0, 2)
+        fold(2 * YM, 2, 5)
+        net.got_twin(2)
+        fold(2 * YM + 1, 2, 5)
+        net.opposite(1)
+        fold(2 * YP, 0, 3)
     fold(2 * YP + 1, 0, 3)
     net.opposite(2)
     net.got_twin(4)
@@ -227,8 +240,8 @@
 
 def kernel(
     scale,
-    columns,
-    count,
+    columns_hbm,
+    count_hbm,
     feat_hbm,
     tiles_hbm,
     weight_hbm,
@@ -236,6 +249,8 @@
     lo_hbm,
     fg_hbm,
     wg_hbm,
+    columns,
+    count,
     kof,
     tiles,
     g1,
@@ -243,8 +258,6 @@
     acc,
     weight,
     og,
-    agg,
-    slope,
     lo,
     fg,
     wp,
@@ -276,6 +289,10 @@
     peers += [shifted(dz=d) for d in range(1, 8)]
     for peer in peers:
         pl.semaphore_signal(barrier, 1, device_id=peer)
+    load_c = pltpu.make_async_copy(columns_hbm, columns, local.at[3])
+    load_n = pltpu.make_async_copy(count_hbm, count, local.at[4])
+    load_c.start()
+    load_n.start()
     load_t.start()
     load_w.start()
     load_o.start()
@@ -286,12 +303,14 @@
     for step in range(CHUNKS):
         net1.own(step)
     tiles[SLOTS] = jnp.zeros((ROWS, ROWS), jnp.bfloat16)
+    load_c.wait()
+    load_n.wait()
     for o, (dp, dy) in enumerate(ORDER):
         for dc in range(2):
             block = ((x // 2 + dp) % 2) * 8 + ((y + dy) % 4) * 2 + (c + dc) % 2
             slot = jnp.int32(SLOTS)
             for k in range(SLOTS - 1, -1, -1):
-                slot = jnp.where((columns[k] == block) & (k < count[0]), k, slot)
+                slot = jnp.where((columns[0, 0, k] == block) & (k < count[0, 0]), k, slot)
             kof[2 * o + dc] = slot
     load_t.wait()
     total = run(net1, tiles, kof, acc, ())
@@ -301,24 +320,19 @@
     for step in range(CHUNKS):
         rows = pl.ds(MADE[step] * CHUNK, CHUNK)
         a = total(rows).astype(jnp.bfloat16)
-        agg[rows, :] = a
         linear = jnp.dot(a, weight[...], preferred_element_type=jnp.float32)
         sig = jax.nn.sigmoid(linear)
         lo[rows, :] = (linear * sig).astype(jnp.bfloat16)
         s = (og[rows, :].astype(jnp.float32) * (sig * (1.0 + linear * (1.0 - sig)))).astype(jnp.bfloat16)
-        slope[rows, :] = s
         g2[0, rows, :] = lax.dot_general(
             s, weight[...], (((1,), (1,)), ((), ())), preferred_element_type=jnp.float32
         ).astype(jnp.bfloat16)
         net2.own(step)
+        term = lax.dot_general(a, s, (((0,), (0,)), ((), ())), preferred_element_type=jnp.float32).reshape(wp.shape)
+        wp[...] = term if step == 0 else wp[...] + term
 
     store_lo = pltpu.make_async_copy(lo, lo_hbm, local.at[0])
     store_lo.start()
-    partial = lax.dot_general(
-        agg[...], slope[...], (((0,), (0,)), ((), ())), preferred_element_type=jnp.float32
-    )
-    wp[...] = partial.reshape(wp.shape)
-
     def put(i, src, dst, target):
         pltpu.make_async_remote_copy(src, dst, wsent.at[0], wrecv.at[i], device_id=target).start()
 
@@ -409,17 +423,17 @@
             jax.ShapeDtypeStruct((ROWS, WIDTH), bf),
             jax.ShapeDtypeStruct((2, 8, 16, WIDTH), bf),
         ),
-        in_specs=[pl.BlockSpec(memory_space=pltpu.SMEM)] * 2 + [any_spec] * 4,
+        in_specs=[any_spec] * 6,
         out_specs=(any_spec, any_spec, any_spec),
         scratch_shapes=[
+            pltpu.SMEM((1, 1, SLOTS), jnp.int32),
+            pltpu.SMEM((1, 1), jnp.int32),
             pltpu.SMEM((16,), jnp.int32),
             pltpu.VMEM((SLOTS + 1, ROWS, ROWS), bf),
             pltpu.VMEM((16, ROWS, WIDTH), bf),
             pltpu.VMEM((16, ROWS, WIDTH), bf),
             pltpu.VMEM((ROWS, WIDTH), f32),
             pltpu.VMEM((WIDTH, WIDTH), bf),
-            pltpu.VMEM((ROWS, WIDTH), bf),
-            pltpu.VMEM((ROWS, WIDTH), bf),
             pltpu.VMEM((ROWS, WIDTH), bf),
             pltpu.VMEM((ROWS, WIDTH), bf),
             pltpu.VMEM((ROWS, WIDTH), bf),
@@ -430,7 +444,7 @@
             pltpu.VMEM((4, 16, WIDTH), bf),
             pltpu.VMEM((4, 16, WIDTH), bf),
             pltpu.VMEM((2, 8, 16, WIDTH), bf),
-            dma((3,)),
+            dma((5,)),
             dma((15,)),
             dma((11,)),
             dma((15,)),
@@ -442,7 +456,7 @@
         compiler_params=pltpu.CompilerParams(
             collective_id=0, has_side_effects=True, vmem_limit_bytes=62 << 20
         ),
-    )(slot_columns[0, 0], slot_counts[0], features[0, 0], tiles[0, 0], weight, out_grad[0, 0])
+    )(slot_columns, slot_counts, features[0, 0], tiles[0, 0], weight, out_grad[0, 0])
     lo, fg, wg = pl.pallas_call(
         hand_out,
         name="hand_out",

time: 60.4 us -> 59.7 us (0.988)
  Pallas kernels: 59 us -> 58.3 us
    pallas_call x1, Pallas kernels: 57.1 us -> 56.4 us  [per_device(): pl.pallas_call(functools.partial(kernel, scale), name='graph_layer', out_...]
where the time goes in v3:
time: 59.7 us; the launch traced here: 59.6 us
  Pallas kernels  58.3 us (98%)
  between operations  1.29 us (2%)
    pallas_call x1, Pallas kernels, per_device(): pl.pallas_call(functools.partial(kernel, scale), name='graph_layer', out_...  56.4 us
    pallas_call x1, Pallas kernels, per_device(): pl.pallas_call(hand_out, name='hand_out', out_shape=(jax.ShapeDtypeStruct...  1.93 us

profile of v3, /device:TPU:1, one launch (start us, length us, event | category | flops | bytes accessed | tf_op | source)
XLA Modules:
  0.0 59.6 jit_solution(8770127956195187866)
XLA Ops:
  1.3 56.4 %graph_layer.1 = (bf16[640,256]{1,0:T(8,128)(2,1)}, bf16[640,256]{1,0:T(8,128)(2,1)}, bf16[2,8,16,256]{3,2,1,0:T(8,128)(2,1)}) custom-call(s32[1,1,8]{2,1,0:T(1,128)} %columns_hbm.1, s32[1,1]{1,0:T(1,128)S(6)} %copy.9.count_hbm, bf16[640,256]{1,0:T(8,128)(2,1)} %bitcast.7, bf16[8,640,640]{2,1,0:T(8,128)(2,1)} %bitcast.6, bf16[256,256]{1,0:T(8,128)(2,1)} %weight_hbm.1, ...), custom_call_target="tpu_custom_call" | custom-call | tf_op jit(solution)/shard_map/graph_layer/pallas_call | solution.py:418
  57.7 1.9 %hand_out.1 = (bf16[640,256]{1,0:T(8,128)(2,1)}, bf16[640,256]{1,0:T(8,128)(2,1)}, f32[256,256]{1,0:T(8,128)}) custom-call(bf16[640,256]{1,0:T(8,128)(2,1)} %get-tuple-element.9.lo, bf16[640,256]{1,0:T(8,128)(2,1)} %get-tuple-element.10.fg, bf16[256,256]{1,0:T(8,128)(2,1)} %bitcast.9), custom_call_target="tpu_custom_call" | custom-call | tf_op jit(solution)/shard_map/hand_out/pallas_call | solution.py:460
